TPU v7x, 512 devices: a whole 4x8x8 slice. The times are simulated.
512 devices in a mesh: row: 64 (over z, x, y_hi), rep: 8 (over y_lo, core).
Axes of the slice: x: 4, y: 8 (y_hi: 2, y_lo: 4; y = y_hi * 4 + y_lo), z: 8, core: 2. Of those that a mesh axis runs over, the one named last changes fastest.
Arguments:
- out_grad: bfloat16 [131072, 256], P(('rep', 'row')), may hold values from -6 to 6
- node_input: bfloat16 [131072, 256], P(('row', 'rep')), may hold values from -0.015625 to 0.015625
- weight: bfloat16 [256, 256], replicated, may hold values from -0.375 to 0.375
- tile_vals: bfloat16 [64, 8, 128, 128, 128], P('row', 'rep'), may hold values from -0.25 to 0.25
- tile_rows: int32 [64, 8, 128], P('row', 'rep'), may hold values from 0 to 15, as said below
- tile_cols: int32 [64, 8, 128], P('row', 'rep'), may hold values from 0 to 127
- tile_count: int32 [64, 8], P('row', 'rep'), may hold values from 32 to 128, as said below
Outputs:
- input_grad: bfloat16 [131072, 256], P(('row', 'rep'))
- weight_grad: float32 [256, 256], replicated
Inputs may be any that keep to these rules, and one draw needn't show every extreme that they name: On one device no pair (tile_rows, tile_cols) repeats among all 128 list entries. `tile_count`: entries at or past a device's count are padding. Some device has exactly 128 live entries in every draw.
All inputs are finite; a program needn't handle non-finite values.
Results may differ from a plain program's by a relative error of at most 0.005.
Values may be sent and summed in bfloat16 or wider, within the bound.
A program may use at most 64 MiB of HBM per device.

v0:
```python
import math

import jax
import jax.numpy as jnp
from jax import lax
from jax.sharding import PartitionSpec as P


def shards(out_grad, node_input, weight, tile_vals, tile_rows, tile_cols, tile_count):
    tile_size = tile_vals.shape[-1]
    features = out_grad.shape[1]
    capacity = tile_vals.shape[2]
    tile_values = tile_vals.reshape(capacity, tile_size, tile_size)
    row_ids = tile_rows.reshape(capacity)
    column_ids = tile_cols.reshape(capacity)
    live_tiles = tile_count.reshape(())
    slab_tiles = node_input.shape[0] * lax.axis_size("rep") // tile_size
    group_tiles = out_grad.shape[0] * lax.axis_size("row") // tile_size
    slab_ids = jnp.arange(slab_tiles, dtype=jnp.int32)
    zero_slab = jnp.zeros((slab_tiles, tile_size, features), jnp.float32)

    def add_block(totals, indices, weights, grad_blocks):
        product = jnp.einsum(
            "tij,tjf->tif",
            jnp.take(tile_values, indices, axis=0),
            grad_blocks,
            preferred_element_type=jnp.float32,
        )
        selector = (jnp.take(row_ids, indices)[:, None] == slab_ids[None, :]).astype(jnp.float32)
        selector = selector * weights[:, None]
        return totals + jnp.einsum(
            "ts,tif->sif", selector, product, precision=lax.Precision.HIGHEST
        )

    block_size = math.gcd(capacity, 32)
    lane_ids = jnp.arange(block_size, dtype=jnp.int32)
    whole = lax.all_gather(out_grad, "row", axis=0, tiled=True)
    group_blocks = whole.reshape(group_tiles, tile_size, features)
    block_count = (live_tiles + block_size - 1) // block_size

    def whole_step(turn, totals):
        indices = turn * block_size + lane_ids
        weights = (indices < live_tiles).astype(jnp.float32)
        grad_blocks = jnp.take(group_blocks, jnp.take(column_ids, indices), axis=0)
        return add_block(totals, indices, weights, grad_blocks)

    partial_slab = lax.fori_loop(0, block_count, whole_step, zero_slab)
    flattened = partial_slab.reshape(slab_tiles * tile_size, features)
    node_grad = lax.psum_scatter(flattened, "rep", scatter_dimension=0, tiled=True)
    local_weight = jnp.dot(
        node_input.astype(jnp.float32).T, node_grad, precision=lax.Precision.HIGHEST
    )
    weight_grad = lax.psum(local_weight, ("row", "rep"))
    node_grad_b = node_grad.astype(jnp.bfloat16)
    input_grad = jnp.einsum(
        "nf,gf->ng", node_grad_b, weight, preferred_element_type=jnp.float32
    ).astype(jnp.bfloat16)
    return (input_grad, weight_grad)


def solution(mesh):
    placed = (
        P(("rep", "row"), None),
        P(("row", "rep"), None),
        P(),
        P("row", "rep", None, None, None),
        P("row", "rep", None),
        P("row", "rep", None),
        P("row", "rep"),
    )
    return jax.shard_map(
        shards,
        mesh=mesh,
        in_specs=placed,
        out_specs=(P(("row", "rep"), None), P()),
        check_vma=False,
    )
```

profile of v0, /device:TPU:1, one launch (start us, length us, event | category | flops | bytes accessed | tf_op | source)
XLA Modules:
  0.0 596.4 jit_solution(9324817699127962845)
XLA Ops:
  7.2 0.0 all-gather.2.cloned.1.call-start
  7.2 0.7 all-gather.2.cloned.1.call-update
  7.9 0.0 reduce-scatter.2.cloned.1.call-start
  8.6 197.7 %all-gather.2.cloned.1.call-done = bf16[16384,256]{1,0:T(8,128)(2,1)} async-done(((bf16[256,256]{1,0:T(8,128)(2,1)}), bf16[16384,256]{1,0:T(8,128)(2,1)}) %all-gather.2.cloned.1.call-update) | async-done | bytes 8388624 | tf_op jit(solution)/shard_map/all_gather | solution.py:37
  206.4 1.6 broadcast_in_dim.34
  208.0 34.9 %while.11 = (s32[]{:T(128)}, f32[16,128,256]{2,0,1:T(8,128)}, s32[]{:T(128)}, s32[128]{0:T(128)S(1)}, s32[]{:T(128)}, /*index=5*/bf16[128,128,128]{2,1,0:T(8,128...) while((s32[]{:T(128)}, f32[16,128,256]{2,0,1:T(8,128)}, s32[]{:T(128)}, ...), condition=%wide.region_1.3_spmd.clone, body=%wide.region_0.2_spmd.clone.sunk | while | flops 471864352 | bytes 38812480 | solution.py:47
  208.0 0.6 compare_convert_fusion.2
  208.7 0.7 gather_fusion.3
  209.4 0.7 gather_fusion
  210.2 2.9 gather_fusion.2
  213.1 4.1 gather_fusion.1
  217.2 0.8 fusion.40
  218.0 0.8 copy-done.3
  218.8 5.3 fusion.41
  224.1 1.4 copy-done.4
  225.5 0.6 compare_convert_fusion.2
  226.2 0.7 gather_fusion.3
  226.9 0.7 gather_fusion
  227.6 2.9 gather_fusion.2
  230.6 4.1 gather_fusion.1
  234.6 0.8 fusion.40
  235.4 0.8 copy-done.3
  236.2 5.3 fusion.41
  241.5 1.4 copy-done.4
  242.9 4.1 copy.10
  247.1 0.0 all-reduce.2.cloned.1.call-start
  247.1 66.1 %reduce-scatter.2.cloned.1.call-done = f32[256,256]{1,0:T(8,128)} async-done(((f32[2048,256]{1,0:T(8,128)}), f32[256,256]{1,0:T(8,128)}) %reduce-scatter.2.cloned.1.call-update) | async-done | bytes 262160 | tf_op jit(solution)/shard_map/reduce_scatter | solution.py:49
  313.3 2.0 convolution_bitcast_fusion
  315.3 0.0 all-reduce.2.cloned.1.call-update
  315.3 1.8 convolution_convert_fusion
  317.2 270.9 %all-reduce.2.cloned.1.call-done = f32[256,256]{0,1:T(8,128)} async-done(((f32[256,256]{0,1:T(8,128)}), f32[256,256]{0,1:T(8,128)}) %all-reduce.2.cloned.1.call-update) | async-done | bytes 262160 | tf_op jit(solution)/shard_map/psum | solution.py:53
  588.1 1.8 copy.11
  (27 shorter events, 0.1 us)
Async XLA Ops:
  7.2 306.1 %copy-start = (bf16[256,256]{1,0:T(8,128)(2,1)S(1)}, bf16[256,256]{1,0:T(8,128)(2,1)}, u32[]{:S(2)}) copy-start(bf16[256,256]{1,0:T(8,128)(2,1)} %param.12) | copy-start | bytes 393220
  7.2 200.8 %copy-start.2 = (s32[1,1,128]{2,1,0:T(1,128)S(1)}, s32[1,1,128]{2,1,0:T(1,128)}, u32[]{:S(2)}) copy-start(s32[1,1,128]{2,1,0:T(1,128)} %param.16) | copy-start | bytes 1540
  7.2 200.8 %copy-start.1 = (s32[1,1,128]{2,1,0:T(1,128)S(1)}, s32[1,1,128]{2,1,0:T(1,128)}, u32[]{:S(2)}) copy-start(s32[1,1,128]{2,1,0:T(1,128)} %param.15) | copy-start | bytes 1540
  7.2 199.2 %all-gather.2.cloned.1.call-start = ((), (), s32[]{:S(2)}) async-start(), calls=%async_computation.1 | async-start | bytes 8519680 | tf_op jit(solution)/shard_map/all_gather | solution.py:37
  7.9 305.3 %reduce-scatter.2.cloned.1.call-start = ((), (), s32[]{:S(2)}) async-start(), calls=%async_computation.2 | async-start | bytes 2359296 | tf_op jit(solution)/shard_map/reduce_scatter | solution.py:49
  217.2 1.6 copy-start.3
  224.1 1.4 copy-start.4
  234.6 1.6 copy-start.3
  241.5 1.4 copy-start.4
  247.0 68.3 %copy-start.5 = (bf16[256,256]{1,0:T(8,128)(2,1)S(1)}, bf16[256,256]{1,0:T(8,128)(2,1)}, u32[]{:S(2)}) copy-start(bf16[256,256]{1,0:T(8,128)(2,1)} %param.13) | copy-start | bytes 393220
  247.1 341.0 %all-reduce.2.cloned.1.call-start = ((), (), s32[]{:S(2)}) async-start(), calls=%async_computation.3 | async-start | bytes 524288 | tf_op jit(solution)/shard_map/psum | solution.py:53
Sparse Core Ops, SparseCore 0:
  12.5 193.8 all-gather.1
  247.2 66.0 reduce-scatter.1
  318.8 269.1 all-reduce.1
where the time goes:
time: 597 us; the launch traced here: 596 us
  waiting for transfers between devices  535 us (90%)
  local copies, waits for them, and re-layouts  28.7 us (5%)
  matrix products  16 us (3%)
  between operations  14.4 us (2%)
    psum x1, waiting for transfers between devices, shards(): weight_grad = lax.psum(local_weight, ('row', 'rep'))  271 us
    all_gather x1, waiting for transfers between devices, shards(): whole = lax.all_gather(out_grad, 'row', axis=0, tiled=True)  198 us
    reduce_scatter x1, waiting for transfers between devices, shards(): lax.psum_scatter(flattened, 'rep', scatter_dimension=0, tiled=True)  66.1 us
  transfers between devices with their start and end apart: 3, of which 3 were waited for; matrix products, arithmetic and copies ran while one was open for 0% of the time, Pallas kernels for 0%

commit v1 on v0

v1 whole, which is shorter than its diff:
```python
import heapq

import jax
import jax.numpy as jnp
from jax import lax
from jax.experimental import pallas as pl
from jax.experimental.pallas import tpu as pltpu
from jax.sharding import PartitionSpec as P

MESH = pl.DeviceIdType.MESH
Z, X, YH, YL, CORES = 8, 4, 2, 4, 2
PLANE = Z * X
Y = YH * YL
TILE = 128
CAP = 128
F = 256
ROWS = 256
UNIT = 16
UNITS = ROWS // UNIT
FIRST = (96, 112)


def gather_edges():
    edges = []

    def chain(rnd, part, axis, base, tie):
        half = (Z if axis == 0 else X) // 2

        def at(k):
            return (base[0] + k, base[1]) if axis == 0 else (base[0], base[1] + k)

        for k in range(1, half + (tie > 0)):
            edges.append((rnd, part, at(k - 1), at(k), axis, 1))
        for k in range(1, half + (tie < 0)):
            edges.append((rnd, part, at(1 - k), at(-k), axis, -1))

    for rnd in (0, 1):
        tie = 1 if rnd == 0 else -1
        chain(rnd, 0, 1, (0, 0), tie)
        for dx in (-1, 0, 1, 2 * tie):
            chain(rnd, 0, 0, (0, dx), 1 if dx in (0, 1) else -1)
        chain(rnd, 1, 0, (0, 0), tie)
        for dz in (-3, -2, -1, 0, 1, 2, 3, 4 * tie):
            chain(rnd, 1, 1, (dz, 0), 1 if 0 <= dz <= 3 else -1)
    return edges


def part_rows(rnd, part):
    return (0, FIRST[rnd]) if part == 0 else (FIRST[rnd], ROWS - FIRST[rnd])


def gather_order(edges):
    kids = {}
    for i, (rnd, part, frm, to, axis, way) in enumerate(edges):
        kids.setdefault((rnd, part, frm), []).append(i)

    def size(i):
        rnd, part, _, to, _, _ = edges[i]
        return 1 + sum(size(j) for j in kids.get((rnd, part, to), []))

    queue = [(0.0, 0, (0, 0, (0, 0)), -1), (0.0, 1, (0, 1, (0, 0)), -1)]
    queue += [(11.0, 2, (1, 0, (0, 0)), -1), (11.0, 3, (1, 1, (0, 0)), -1)]
    free, count, order = {}, 4, []
    while queue:
        now, _, node, via = heapq.heappop(queue)
        starts = sorted(kids.get(node, []), key=lambda i: -size(i))
        order.append((node, via, starts))
        for i in starts:
            rnd, part, _, to, axis, way = edges[i]
            begin = max(now, free.get((axis, way), 0.0))
            end = begin + part_rows(rnd, part)[1] * 0.01024
            free[(axis, way)] = end
            heapq.heappush(queue, (end + 1.0, count, (rnd, part, to), i))
            count += 1
    return order


EDGES = gather_edges()
ORDER = gather_order(EDGES)


def schedule(rows_ref, cols_ref, count_ref, meta_ref):
    lane = lax.broadcasted_iota(jnp.int32, (TILE, TILE), 1)
    sub = lax.broadcasted_iota(jnp.int32, (TILE, TILE), 0)

    def wide(value):
        return jnp.broadcast_to(value, (TILE, TILE))

    live = lane < wide(count_ref[...])
    row = jnp.where(live, wide(rows_ref[...]), 16)
    key = row * CAP + lane
    row_t, key_t, col_t = row.T, key.T, wide(cols_ref[...]).T

    def total(value):
        return jnp.sum(value, axis=0, keepdims=True)

    rank = total((key_t < key).astype(jnp.int32))
    match = wide(rank).T == lane
    order = total(jnp.where(match, sub, 0))
    col = total(jnp.where(match, col_t, 0))
    sorted_row = total(jnp.where(match, row_t, 0))
    first = total((row_t < sorted_row).astype(jnp.int32)) == lane[:1]
    upto = total((row_t <= lane).astype(jnp.int32))
    has = total((row_t == lane).astype(jnp.int32))
    slot = jnp.where(has > 0, upto, 0)
    meta_ref[0:1, :] = order
    meta_ref[1:2, :] = col
    meta_ref[2:3, :] = jnp.where(first, 0, lane[:1])
    meta_ref[3:4, :] = slot
    meta_ref[4:8, :] = jnp.zeros((4, TILE), jnp.int32)


def kernel(
    grad_ref, node_ref, weight_ref, vals_ref, meta_s,
    dx_ref, dw_ref,
    grads, tiles, sums, high, low, nodes, nodes_t, sib, outgoing, incoming,
    w_part, w_sib, w_half, w_plane, w_unit, w_y, w_full,
    local_sem, gs_sem, gr_sem, ys_sem, yr_sem, ns_sem, nr_sem, ss_sem, sr_sem,
    rs_sem, rr_sem, w0_sem, p1s_sem, p1r_sem, us_sem, ur_sem, p2s_sem, p2r_sem, w4_sem,
):
    me = lax.axis_index("row")
    rep = lax.axis_index("rep")
    z, x, yh = me // (X * YH), (me // YH) % X, me % YH
    yl, core = rep // CORES, rep % CORES
    y = yh * YL + yl
    u = z * X + x
    sibling = (me, rep + 1 - 2 * core)

    def plane_peer(k):
        return ((u + k) % PLANE * YH + yh, rep)

    def y_peer(k):
        other = (y + k) % Y
        return (u * YH + other // YL, other % YL * CORES + core)

    def rep_peer(k):
        return (me, (yl + k) % YL * CORES + core)

    own_copies = [
        pltpu.make_async_copy(grad_ref, grads.at[pl.ds(me * UNITS, UNITS)], local_sem.at[0]),
        pltpu.make_async_copy(node_ref, nodes.at[rep], local_sem.at[1]),
        pltpu.make_async_copy(vals_ref, tiles, local_sem.at[2]),
    ]
    for copy in own_copies:
        copy.start()

    barrier = pltpu.get_barrier_semaphore()

    def greet(k, carry):
        pl.semaphore_signal(barrier, inc=1, device_id=plane_peer(k), device_id_type=MESH)
        return carry

    lax.fori_loop(1, PLANE, greet, 0)
    for k in range(1, Y):
        pl.semaphore_signal(barrier, inc=1, device_id=y_peer(k), device_id_type=MESH)
    pl.semaphore_signal(barrier, inc=1, device_id=sibling, device_id_type=MESH)
    pl.semaphore_wait(barrier, PLANE - 1 + Y - 1 + 1)

    def piece(rnd, part, offset):
        pz, px = (z - offset[0] + Z) % Z, (x - offset[1] + X) % X
        py = yh if rnd == 0 else 1 - yh
        begin, size = part_rows(rnd, part)
        return grads.at[pl.ds(((pz * X + px) * YH + py) * UNITS + begin // UNIT, size // UNIT)]

    def hop(i, landed):
        rnd, part, frm, to, axis, way = EDGES[i]
        ref = piece(rnd, part, to if landed else frm)
        nz = (z + way + Z) % Z if axis == 0 else z
        nx = (x + way + X) % X if axis == 1 else x
        return pltpu.make_async_remote_copy(
            src_ref=ref, dst_ref=ref, send_sem=gs_sem.at[i], recv_sem=gr_sem.at[i],
            device_id=((nz * X + nx) * YH + yh, rep), device_id_type=MESH,
        )

    own_copies[0].wait()
    partner = ((u * YH) + 1 - yh, rep)

    def across(index):
        ref = grads.at[pl.ds((u * YH + index) * UNITS, UNITS)]
        return pltpu.make_async_remote_copy(
            src_ref=ref, dst_ref=ref, send_sem=ys_sem.at[0], recv_sem=yr_sem.at[0],
            device_id=partner, device_id_type=MESH,
        )

    sent = []
    for step, (node, via, starts) in enumerate(ORDER):
        if not starts:
            continue
        if via >= 0:
            hop(via, True).wait_recv()
        elif node == (1, 0, (0, 0)):
            across(1 - yh).wait_recv()
        for i in starts:
            copy = hop(i, False)
            copy.start()
            sent.append(copy)
        if step == 1:
            across_copy = across(yh)
            across_copy.start()
            own_copies[1].wait()

            def node_copy(k, landed):
                block = nodes.at[rep_peer(YL - k)[1] if landed else rep]
                return pltpu.make_async_remote_copy(
                    src_ref=block, dst_ref=block, send_sem=ns_sem.at[k], recv_sem=nr_sem.at[k],
                    device_id=rep_peer(k), device_id_type=MESH,
                )

            def node_pass(k, landed):
                source = rep_peer(YL - k)[1]
                block = nodes.at[source + 1 - 2 * core if landed else source]
                return pltpu.make_async_remote_copy(
                    src_ref=block, dst_ref=block, send_sem=ns_sem.at[YL + k], recv_sem=nr_sem.at[YL + k],
                    device_id=sibling, device_id_type=MESH,
                )

            node_sent = [node_copy(k, False) for k in range(1, YL)] + [node_pass(0, False)]
            for copy in node_sent:
                copy.start()
            sums[0] = jnp.zeros((TILE, F), jnp.float32)

    for k in range(1, YL):
        node_copy(k, True).wait_recv()
        copy = node_pass(k, False)
        copy.start()
        node_sent.append(copy)
    for k in range(YL):
        node_pass(k, True).wait_recv()
    for q in range(YL * CORES):
        nodes_t[:, q * ROWS:(q + 1) * ROWS] = nodes[q].T
    own_copies[2].wait()
    for node, via, starts in ORDER:
        if not starts:
            hop(via, True).wait_recv()

    def tile_step(i, carry):
        unit = meta_s[1, i] * (TILE // UNIT)
        block = jnp.concatenate([grads[unit + j] for j in range(TILE // UNIT)], axis=0)
        product = jnp.dot(tiles[meta_s[0, i]], block, preferred_element_type=jnp.float32)
        sums[i + 1] = sums[meta_s[2, i]] + product
        return carry

    lax.fori_loop(0, CAP, tile_step, 0, unroll=8)

    def take_sum(s, carry):
        total = sums[meta_s[3, s]]
        top = total.astype(jnp.bfloat16)
        at = pl.ds(pl.multiple_of(s * TILE, TILE), TILE)
        high[at] = top
        low[at] = (total - top.astype(jnp.float32)).astype(jnp.bfloat16)
        return carry

    lax.fori_loop(0, 16, take_sum, 0, unroll=2)

    def block_of(index):
        return pl.ds(pl.multiple_of(index * ROWS, ROWS), ROWS)

    def sib_copy(k):
        dest = (yl + k) % YL
        return pltpu.make_async_remote_copy(
            src_ref=high.at[block_of(dest * CORES + 1 - core)], dst_ref=sib.at[dest],
            send_sem=ss_sem.at[k], recv_sem=sr_sem.at[k], device_id=sibling, device_id_type=MESH,
        )

    sib_sent = [sib_copy(k) for k in (2, 1, 3, 0)]
    for copy in sib_sent:
        copy.start()

    def w_dot(half):
        left = nodes_t[pl.ds(pl.multiple_of(half * TILE, TILE), TILE)]
        term = jnp.dot(left, high[...], preferred_element_type=jnp.float32)
        term += jnp.dot(left, low[...], preferred_element_type=jnp.float32)
        for h in range(2):
            w_part[half, h * 16:(h + 1) * 16] = term[:, h * TILE:(h + 1) * TILE].reshape(16, 8, TILE)

    w_dot(1 - core)
    w_copy = pltpu.make_async_remote_copy(
        src_ref=w_part.at[1 - core], dst_ref=w_sib, send_sem=w0_sem.at[0], recv_sem=w0_sem.at[1],
        device_id=sibling, device_id_type=MESH,
    )
    w_copy.start()
    w_dot(core)

    def both(index, at):
        rows = block_of(index)
        return high[rows].astype(jnp.float32) + low[rows].astype(jnp.float32) + sib[at].astype(jnp.float32)

    def out_copy(k):
        return pltpu.make_async_remote_copy(
            src_ref=outgoing.at[k], dst_ref=incoming.at[k], send_sem=rs_sem.at[k], recv_sem=rr_sem.at[k],
            device_id=rep_peer(k), device_id_type=MESH,
        )

    w_copy.wait_recv()
    w_half[...] = w_part[core] + w_sib[...]

    def plane_send(k, carry):
        pltpu.make_async_remote_copy(
            src_ref=w_half.at[(u + k) % PLANE], dst_ref=w_plane.at[k],
            send_sem=p1s_sem.at[k], recv_sem=p1r_sem.at[k], device_id=plane_peer(k), device_id_type=MESH,
        ).start()
        return carry

    lax.fori_loop(1, PLANE, plane_send, 0)
    for k in (2, 1, 3):
        sib_copy(k).wait_recv()
        dest = (yl + k) % YL
        outgoing[k] = both(dest * CORES + core, dest).astype(jnp.bfloat16)
        out_copy(k).start()

    def plane_sum(k, total):
        pltpu.make_async_remote_copy(
            src_ref=w_half.at[(u + k) % PLANE], dst_ref=w_plane.at[k],
            send_sem=p1s_sem.at[k], recv_sem=p1r_sem.at[k], device_id=plane_peer(k), device_id_type=MESH,
        ).wait_recv()
        return total + w_plane[k]

    w_unit[y] = lax.fori_loop(1, PLANE, plane_sum, w_half[u])

    def y_copy(k, landed):
        slot = (y + Y - k) % Y if landed else y
        return pltpu.make_async_remote_copy(
            src_ref=w_unit.at[y], dst_ref=w_unit.at[slot],
            send_sem=us_sem.at[k], recv_sem=ur_sem.at[k], device_id=y_peer(k), device_id_type=MESH,
        )

    y_sent = [y_copy(k, False) for k in (4, 3, 5, 2, 6, 1, 7)]
    for copy in y_sent:
        copy.start()
    for k in range(1, Y):
        y_copy(k, True).wait_recv()
    total = w_unit[0]
    for k in range(1, Y):
        total += w_unit[k]
    w_full[core, u] = total

    def spread(k, landed):
        unit = w_full.at[core, (u + PLANE - k) % PLANE if landed else u]
        return pltpu.make_async_remote_copy(
            src_ref=unit, dst_ref=unit,
            send_sem=p2s_sem.at[k], recv_sem=p2r_sem.at[k], device_id=plane_peer(k), device_id_type=MESH,
        )

    def spread_start(k, carry):
        spread(k, False).start()
        return carry

    def spread_wait(k, carry):
        spread(k, True).wait_recv()
        return carry

    lax.fori_loop(1, PLANE, spread_start, 0)
    lax.fori_loop(1, PLANE, spread_wait, 0)

    def last_copy(index):
        return pltpu.make_async_remote_copy(
            src_ref=w_full.at[index], dst_ref=w_full.at[index], send_sem=w4_sem.at[0], recv_sem=w4_sem.at[1],
            device_id=sibling, device_id_type=MESH,
        )

    final = last_copy(core)
    final.start()

    sib_copy(0).wait_recv()
    node_grad = both(rep, yl)
    for k in range(1, YL):
        out_copy(k).wait_recv()
        node_grad += incoming[k].astype(jnp.float32)
    dx_ref[...] = lax.dot_general(
        node_grad.astype(jnp.bfloat16), weight_ref[...], (((1,), (1,)), ((), ())),
        preferred_element_type=jnp.float32,
    ).astype(jnp.bfloat16)

    last_copy(1 - core).wait_recv()
    for half in range(2):
        for h in range(2):
            dw_ref[half * TILE:(half + 1) * TILE, h * TILE:(h + 1) * TILE] = (
                w_full[half, h * 16:(h + 1) * 16].reshape(TILE, TILE)
            )

    for copy in sent + [across_copy] + node_sent + sib_sent + [w_copy, final] + y_sent:
        copy.wait_send()
    for k in range(1, YL):
        out_copy(k).wait_send()

    def drain(k, carry):
        pltpu.make_async_remote_copy(
            src_ref=w_half.at[(u + k) % PLANE], dst_ref=w_plane.at[k],
            send_sem=p1s_sem.at[k], recv_sem=p1r_sem.at[k], device_id=plane_peer(k), device_id_type=MESH,
        ).wait_send()
        spread(k, False).wait_send()
        return carry

    lax.fori_loop(1, PLANE, drain, 0)


def shards(out_grad, node_input, weight, tile_vals, tile_rows, tile_cols, tile_count):
    vmem = pl.BlockSpec(memory_space=pltpu.VMEM)
    hbm = pl.BlockSpec(memory_space=pl.ANY)
    f32, bf16 = jnp.float32, jnp.bfloat16
    dma = pltpu.SemaphoreType.DMA
    slab = YL * CORES * ROWS
    meta = pl.pallas_call(
        schedule,
        out_shape=jax.ShapeDtypeStruct((8, TILE), jnp.int32),
        in_specs=[vmem] * 3,
        out_specs=vmem,
    )(tile_rows.reshape(1, CAP), tile_cols.reshape(1, CAP), tile_count.reshape(1, 1))
    return pl.pallas_call(
        kernel,
        out_shape=(
            jax.ShapeDtypeStruct((ROWS, F), bf16),
            jax.ShapeDtypeStruct((F, F), f32),
        ),
        in_specs=[hbm, hbm, vmem, hbm, pl.BlockSpec(memory_space=pltpu.SMEM)],
        out_specs=(vmem, vmem),
        scratch_shapes=[
            pltpu.VMEM((PLANE * YH * UNITS, UNIT, F), bf16),
            pltpu.VMEM((CAP, TILE, TILE), bf16),
            pltpu.VMEM((CAP + 1, TILE, F), f32),
            pltpu.VMEM((slab, F), bf16),
            pltpu.VMEM((slab, F), bf16),
            pltpu.VMEM((YL * CORES, ROWS, F), bf16),
            pltpu.VMEM((F, slab), bf16),
            pltpu.VMEM((YL, ROWS, F), bf16),
            pltpu.VMEM((YL, ROWS, F), bf16),
            pltpu.VMEM((YL, ROWS, F), bf16),
            pltpu.VMEM((2, PLANE, 8, TILE), f32),
            pltpu.VMEM((PLANE, 8, TILE), f32),
            pltpu.VMEM((PLANE, 8, TILE), f32),
            pltpu.VMEM((PLANE, 8, TILE), f32),
            pltpu.VMEM((Y, 8, TILE), f32),
            pltpu.VMEM((Y, 8, TILE), f32),
            pltpu.VMEM((2, PLANE, 8, TILE), f32),
            dma((3,)),
            dma((len(EDGES),)), dma((len(EDGES),)),
            dma((1,)), dma((1,)),
            dma((2 * YL,)), dma((2 * YL,)),
            dma((YL,)), dma((YL,)),
            dma((YL,)), dma((YL,)),
            dma((2,)),
            dma((PLANE,)), dma((PLANE,)),
            dma((Y,)), dma((Y,)),
            dma((PLANE,)), dma((PLANE,)),
            dma((2,)),
        ],
        compiler_params=pltpu.CompilerParams(
            collective_id=0, has_side_effects=True, vmem_limit_bytes=48 * 1024 * 1024
        ),
        cost_estimate=pl.CostEstimate(flops=2_000_000_000, bytes_accessed=5_000_000, transcendentals=0),
    )(
        out_grad.reshape(UNITS, UNIT, F),
        node_input,
        weight,
        tile_vals.reshape(CAP, TILE, TILE),
        meta,
    )


def solution(mesh):
    placed = (
        P(("rep", "row"), None),
        P(("row", "rep"), None),
        P(),
        P("row", "rep", None, None, None),
        P("row", "rep", None),
        P("row", "rep", None),
        P("row", "rep"),
    )
    return jax.shard_map(
        shards,
        mesh=mesh,
        in_specs=placed,
        out_specs=(P(("row", "rep"), None), P()),
        check_vma=False,
    )
```

time: 597 us -> 115 us (0.19)
  waiting for transfers between devices: 535 us -> 0 us
  Pallas kernels: 0 us -> 107 us
  local copies, waits for them, and re-layouts: 28.7 us -> 6.94 us
  matrix products: 16 us -> 0 us
  between operations: 14.4 us -> 1.29 us
    psum x1 -> x0, waiting for transfers between devices: 271 us -> none  [shards(): weight_grad = lax.psum(local_weight, ('row', 'rep'))]
    all_gather x1 -> x0, waiting for transfers between devices: 198 us -> none  [shards(): whole = lax.all_gather(out_grad, 'row', axis=0, tiled=True)]
    pallas_call x0 -> x2, Pallas kernels: none -> 107 us  [the longest x1 105 us: shards(): pl.pallas_call(kernel, out_shape=(jax.ShapeDtypeStruct((ROWS, F), bf16),...]
    reduce_scatter x1 -> x0, waiting for transfers between devices: 66.1 us -> none  [shards(): lax.psum_scatter(flattened, 'rep', scatter_dimension=0, tiled=True)]
    gather x8 -> x0, local copies, waits for them, and re-layouts: 16.8 us -> none  [the longest x4 9.53 us: whole_step(): grad_blocks = jnp.take(group_blocks, jnp.take(column_ids, indices), axis=0)]
    dot_general x6 -> x0, matrix products: 16 us -> none  [the longest x2 10.6 us: add_block(): jnp.einsum('ts,tif->sif', selector, product, precision=lax.Precision.HIGH...]
    while x9 -> x0, local copies, waits for them, and re-layouts: 8.46 us -> none
  transfers between devices with their start and end apart: 3 -> 0, of which waited for: 3 -> 0; matrix products, arithmetic and copies ran while one was open for 0% -> 0% of each run, Pallas kernels for 0% -> 0%
where the time goes in v1:
time: 115 us
  Pallas kernels  107 us (93%)
  local copies, waits for them, and re-layouts  6.94 us (6%)
  between operations  1.29 us (1%)
    pallas_call x1, Pallas kernels, shards(): pl.pallas_call(kernel, out_shape=(jax.ShapeDtypeStruct((ROWS, F), bf16),...  105 us
    unnamed x12, local copies, waits for them, and re-layouts  6.94 us

profile of v1, /device:TPU:1, one launch (start us, length us, event | category | flops | bytes accessed | tf_op | source)
XLA Modules:
  0.0 114.8 jit_solution(2810244179695588770)
XLA Ops:
  1.3 1.6 %shard_map.86.meta_s = s32[8,128]{1,0:T(8,128)} custom-call(s32[1,128]{1,0:T(1,128)} %bitcast.6, s32[1,128]{1,0:T(1,128)} %bitcast.7, s32[1,1]{1,0:T(1,128)S(6)} %copy.11.count_ref), custom_call_target="tpu_custom_call" | custom-call | tf_op jit(solution)/shard_map/pallas_call | solution.py:403
  2.9 0.0 copy-start
  2.9 0.7 copy-done
  3.6 0.0 copy-start.1
  3.6 2.2 %copy-done.1 = bf16[1,1,128,128,128]{4,3,2,1,0:T(8,128)(2,1)S(1)} copy-done((bf16[1,1,128,128,128]{4,3,2,1,0:T(8,128)(2,1)S(1)}, bf16[1,1,128,128,128]{4,3,2,1,0:T(8,128)(2,1)}, u32[]{:S(2)}) %copy-start.1) | copy-done | bytes 4194328
  5.8 0.0 copy-start.2
  5.8 0.9 copy-done.2
  6.7 0.0 copy-start.3
  6.7 0.9 copy-done.3
  7.6 0.0 copy-start.4
  7.6 0.9 copy-done.4
  8.5 105.0 %shard_map.87 = (bf16[256,256]{1,0:T(8,128)(2,1)S(1)}, f32[256,256]{1,0:T(8,128)S(1)}) custom-call(bf16[16,16,256]{2,1,0:T(8,128)(2,1)S(1)} %bitcast.5, bf16[256,256]{1,0:T(8,128)(2,1)S(1)} %copy-done.3, bf16[256,256]{1,0:T(8,128)(2,1)S(1)} %copy-done.4, bf16[128,128,128]{2,1,0:T(8,128)(2,1)S(1)} %bitcast.4, s32[8,128]{1,0:T(8,128)S(1)} %copy-done), custom_call_target="tpu_custom_call" | custom-call | flops 2000000000 | bytes 5000000 | tf_op jit(solution)/shard_map/pallas_call | solution.py:409
  113.5 0.7 copy.12
  114.1 0.7 copy.13
Async XLA Ops:
  2.9 0.7 copy-start
  3.6 2.2 %copy-start.1 = (bf16[1,1,128,128,128]{4,3,2,1,0:T(8,128)(2,1)S(1)}, bf16[1,1,128,128,128]{4,3,2,1,0:T(8,128)(2,1)}, u32[]{:S(2)}) copy-start(bf16[1,1,128,128,128]{4,3,2,1,0:T(8,128)(2,1)} %param.10) | copy-start | bytes 12582916
  5.8 0.9 copy-start.2
  6.7 0.9 copy-start.3
  7.6 0.9 copy-start.4

commit v2 on v1

--- a/solution.py
+++ b/solution.py
@@ -18,6 +18,8 @@
 UNIT = 16
 UNITS = ROWS // UNIT
 FIRST = (96, 112)
+ACROSS_US = 16.0
+LINK_FROM, LINK_STEPS = 12, 16
 
 
 def gather_edges():
@@ -59,7 +61,7 @@
         return 1 + sum(size(j) for j in kids.get((rnd, part, to), []))
 
     queue = [(0.0, 0, (0, 0, (0, 0)), -1), (0.0, 1, (0, 1, (0, 0)), -1)]
-    queue += [(11.0, 2, (1, 0, (0, 0)), -1), (11.0, 3, (1, 1, (0, 0)), -1)]
+    queue += [(ACROSS_US, 2, (1, 0, (0, 0)), -1), (ACROSS_US, 3, (1, 1, (0, 0)), -1)]
     free, count, order = {}, 4, []
     while queue:
         now, _, node, via = heapq.heappop(queue)
@@ -79,42 +81,11 @@
 ORDER = gather_order(EDGES)
 
 
-def schedule(rows_ref, cols_ref, count_ref, meta_ref):
-    lane = lax.broadcasted_iota(jnp.int32, (TILE, TILE), 1)
-    sub = lax.broadcasted_iota(jnp.int32, (TILE, TILE), 0)
-
-    def wide(value):
-        return jnp.broadcast_to(value, (TILE, TILE))
-
-    live = lane < wide(count_ref[...])
-    row = jnp.where(live, wide(rows_ref[...]), 16)
-    key = row * CAP + lane
-    row_t, key_t, col_t = row.T, key.T, wide(cols_ref[...]).T
-
-    def total(value):
-        return jnp.sum(value, axis=0, keepdims=True)
-
-    rank = total((key_t < key).astype(jnp.int32))
-    match = wide(rank).T == lane
-    order = total(jnp.where(match, sub, 0))
-    col = total(jnp.where(match, col_t, 0))
-    sorted_row = total(jnp.where(match, row_t, 0))
-    first = total((row_t < sorted_row).astype(jnp.int32)) == lane[:1]
-    upto = total((row_t <= lane).astype(jnp.int32))
-    has = total((row_t == lane).astype(jnp.int32))
-    slot = jnp.where(has > 0, upto, 0)
-    meta_ref[0:1, :] = order
-    meta_ref[1:2, :] = col
-    meta_ref[2:3, :] = jnp.where(first, 0, lane[:1])
-    meta_ref[3:4, :] = slot
-    meta_ref[4:8, :] = jnp.zeros((4, TILE), jnp.int32)
-
-
 def kernel(
-    grad_ref, node_ref, weight_ref, vals_ref, meta_s,
+    grad_ref, node_ref, weight_ref, vals_ref, rows_ref, cols_ref, count_ref,
     dx_ref, dw_ref,
     grads, tiles, sums, high, low, nodes, nodes_t, sib, outgoing, incoming,
-    w_part, w_sib, w_half, w_plane, w_unit, w_y, w_full,
+    w_part, w_sib, w_half, w_plane, w_unit, w_y, w_full, weights, earlier, latest,
     local_sem, gs_sem, gr_sem, ys_sem, yr_sem, ns_sem, nr_sem, ss_sem, sr_sem,
     rs_sem, rr_sem, w0_sem, p1s_sem, p1r_sem, us_sem, ur_sem, p2s_sem, p2r_sem, w4_sem,
 ):
@@ -140,6 +111,7 @@
         pltpu.make_async_copy(grad_ref, grads.at[pl.ds(me * UNITS, UNITS)], local_sem.at[0]),
         pltpu.make_async_copy(node_ref, nodes.at[rep], local_sem.at[1]),
         pltpu.make_async_copy(vals_ref, tiles, local_sem.at[2]),
+        pltpu.make_async_copy(weight_ref, weights, local_sem.at[3]),
     ]
     for copy in own_copies:
         copy.start()
@@ -172,6 +144,15 @@
             device_id=((nz * X + nx) * YH + yh, rep), device_id_type=MESH,
         )
 
+    def link(t, carry):
+        row = rows_ref[0, t]
+        earlier[t] = latest[row]
+        live = (t < count_ref[0, 0]).astype(jnp.int32)
+        for s in range(16):
+            now = latest[s]
+            latest[s] = now + (row == s).astype(jnp.int32) * live * (t + 1 - now)
+        return carry
+
     own_copies[0].wait()
     partner = ((u * YH) + 1 - yh, rep)
 
@@ -182,10 +163,24 @@
             device_id=partner, device_id_type=MESH,
         )
 
+    def node_copy(k, landed):
+        block = nodes.at[rep_peer(YL - k)[1] if landed else rep]
+        return pltpu.make_async_remote_copy(
+            src_ref=block, dst_ref=block, send_sem=ns_sem.at[k], recv_sem=nr_sem.at[k],
+            device_id=rep_peer(k), device_id_type=MESH,
+        )
+
+    def node_pass(k, landed):
+        source = rep_peer(YL - k)[1]
+        block = nodes.at[source + 1 - 2 * core if landed else source]
+        return pltpu.make_async_remote_copy(
+            src_ref=block, dst_ref=block, send_sem=ns_sem.at[YL + k], recv_sem=nr_sem.at[YL + k],
+            device_id=sibling, device_id_type=MESH,
+        )
+
+    node_sent = [node_copy(k, False) for k in range(1, YL)] + [node_pass(0, False)]
     sent = []
-    for step, (node, via, starts) in enumerate(ORDER):
-        if not starts:
-            continue
+    for step, (node, via, starts) in enumerate([entry for entry in ORDER if entry[2]]):
         if via >= 0:
             hop(via, True).wait_recv()
         elif node == (1, 0, (0, 0)):
@@ -198,26 +193,15 @@
             across_copy = across(yh)
             across_copy.start()
             own_copies[1].wait()
-
-            def node_copy(k, landed):
-                block = nodes.at[rep_peer(YL - k)[1] if landed else rep]
-                return pltpu.make_async_remote_copy(
-                    src_ref=block, dst_ref=block, send_sem=ns_sem.at[k], recv_sem=nr_sem.at[k],
-                    device_id=rep_peer(k), device_id_type=MESH,
-                )
-
-            def node_pass(k, landed):
-                source = rep_peer(YL - k)[1]
-                block = nodes.at[source + 1 - 2 * core if landed else source]
-                return pltpu.make_async_remote_copy(
-                    src_ref=block, dst_ref=block, send_sem=ns_sem.at[YL + k], recv_sem=nr_sem.at[YL + k],
-                    device_id=sibling, device_id_type=MESH,
-                )
-
-            node_sent = [node_copy(k, False) for k in range(1, YL)] + [node_pass(0, False)]
+            for row in range(16):
+                latest[row] = 0
+            sums[0] = jnp.zeros((TILE, F), jnp.float32)
+        elif node == (1, 1, (0, 0)):
             for copy in node_sent:
                 copy.start()
-            sums[0] = jnp.zeros((TILE, F), jnp.float32)
+        if LINK_FROM <= step < LINK_FROM + LINK_STEPS:
+            begin = (step - LINK_FROM) * (CAP // LINK_STEPS)
+            lax.fori_loop(begin, begin + CAP // LINK_STEPS, link, 0)
 
     for k in range(1, YL):
         node_copy(k, True).wait_recv()
@@ -234,16 +218,16 @@
             hop(via, True).wait_recv()
 
     def tile_step(i, carry):
-        unit = meta_s[1, i] * (TILE // UNIT)
+        unit = cols_ref[0, i] * (TILE // UNIT)
         block = jnp.concatenate([grads[unit + j] for j in range(TILE // UNIT)], axis=0)
-        product = jnp.dot(tiles[meta_s[0, i]], block, preferred_element_type=jnp.float32)
-        sums[i + 1] = sums[meta_s[2, i]] + product
+        product = jnp.dot(tiles[i], block, preferred_element_type=jnp.float32)
+        sums[i + 1] = sums[earlier[i]] + product
         return carry
 
     lax.fori_loop(0, CAP, tile_step, 0, unroll=8)
 
     def take_sum(s, carry):
-        total = sums[meta_s[3, s]]
+        total = sums[latest[s]]
         top = total.astype(jnp.bfloat16)
         at = pl.ds(pl.multiple_of(s * TILE, TILE), TILE)
         high[at] = top
@@ -291,6 +275,13 @@
             device_id=rep_peer(k), device_id_type=MESH,
         )
 
+    def send_block(k):
+        sib_copy(k).wait_recv()
+        dest = (yl + k) % YL
+        outgoing[k] = both(dest * CORES + core, dest).astype(jnp.bfloat16)
+        out_copy(k).start()
+
+    send_block(2)
     w_copy.wait_recv()
     w_half[...] = w_part[core] + w_sib[...]
 
@@ -302,11 +293,8 @@
         return carry
 
     lax.fori_loop(1, PLANE, plane_send, 0)
-    for k in (2, 1, 3):
-        sib_copy(k).wait_recv()
-        dest = (yl + k) % YL
-        outgoing[k] = both(dest * CORES + core, dest).astype(jnp.bfloat16)
-        out_copy(k).start()
+    for copy in sent + [across_copy] + node_sent:
+        copy.wait_send()
 
     def plane_sum(k, total):
         pltpu.make_async_remote_copy(
@@ -327,6 +315,8 @@
     y_sent = [y_copy(k, False) for k in (4, 3, 5, 2, 6, 1, 7)]
     for copy in y_sent:
         copy.start()
+    for k in (1, 3):
+        send_block(k)
     for k in range(1, Y):
         y_copy(k, True).wait_recv()
     total = w_unit[0]
@@ -361,13 +351,14 @@
     final = last_copy(core)
     final.start()
 
+    own_copies[3].wait()
     sib_copy(0).wait_recv()
     node_grad = both(rep, yl)
     for k in range(1, YL):
         out_copy(k).wait_recv()
         node_grad += incoming[k].astype(jnp.float32)
     dx_ref[...] = lax.dot_general(
-        node_grad.astype(jnp.bfloat16), weight_ref[...], (((1,), (1,)), ((), ())),
+        node_grad.astype(jnp.bfloat16), weights[...], (((1,), (1,)), ((), ())),
         preferred_element_type=jnp.float32,
     ).astype(jnp.bfloat16)
 
@@ -378,7 +369,7 @@
                 w_full[half, h * 16:(h + 1) * 16].reshape(TILE, TILE)
             )
 
-    for copy in sent + [across_copy] + node_sent + sib_sent + [w_copy, final] + y_sent:
+    for copy in sib_sent + [w_copy, final] + y_sent:
         copy.wait_send()
     for k in range(1, YL):
         out_copy(k).wait_send()
@@ -400,19 +391,13 @@
     f32, bf16 = jnp.float32, jnp.bfloat16
     dma = pltpu.SemaphoreType.DMA
     slab = YL * CORES * ROWS
-    meta = pl.pallas_call(
-        schedule,
-        out_shape=jax.ShapeDtypeStruct((8, TILE), jnp.int32),
-        in_specs=[vmem] * 3,
-        out_specs=vmem,
-    )(tile_rows.reshape(1, CAP), tile_cols.reshape(1, CAP), tile_count.reshape(1, 1))
     return pl.pallas_call(
         kernel,
         out_shape=(
             jax.ShapeDtypeStruct((ROWS, F), bf16),
             jax.ShapeDtypeStruct((F, F), f32),
         ),
-        in_specs=[hbm, hbm, vmem, hbm, pl.BlockSpec(memory_space=pltpu.SMEM)],
+        in_specs=[hbm] * 4 + [pl.BlockSpec(memory_space=pltpu.SMEM)] * 3,
         out_specs=(vmem, vmem),
         scratch_shapes=[
             pltpu.VMEM((PLANE * YH * UNITS, UNIT, F), bf16),
@@ -432,7 +417,10 @@
             pltpu.VMEM((Y, 8, TILE), f32),
             pltpu.VMEM((Y, 8, TILE), f32),
             pltpu.VMEM((2, PLANE, 8, TILE), f32),
-            dma((3,)),
+            pltpu.VMEM((F, F), bf16),
+            pltpu.SMEM((CAP,), jnp.int32),
+            pltpu.SMEM((16,), jnp.int32),
+            dma((4,)),
             dma((len(EDGES),)), dma((len(EDGES),)),
             dma((1,)), dma((1,)),
             dma((2 * YL,)), dma((2 * YL,)),
@@ -445,7 +433,7 @@
             dma((2,)),
         ],
         compiler_params=pltpu.CompilerParams(
-            collective_id=0, has_side_effects=True, vmem_limit_bytes=48 * 1024 * 1024
+            collective_id=0, has_side_effects=True, vmem_limit_bytes=62 * 1024 * 1024
         ),
         cost_estimate=pl.CostEstimate(flops=2_000_000_000, bytes_accessed=5_000_000, transcendentals=0),
     )(
@@ -453,7 +441,9 @@
         node_input,
         weight,
         tile_vals.reshape(CAP, TILE, TILE),
-        meta,
+        tile_rows.reshape(1, CAP),
+        tile_cols.reshape(1, CAP),
+        tile_count.reshape(1, 1),
     )
 
 

time: 115 us -> 105 us (0.913)
  Pallas kernels: 107 us -> 100 us
  local copies, waits for them, and re-layouts: 6.94 us -> 3.24 us
    pallas_call x1, Pallas kernels: 105 us -> 100 us  [shards(): pl.pallas_call(kernel, out_shape=(jax.ShapeDtypeStruct((ROWS, F), bf16),...]
    unnamed x12 -> x2, local copies, waits for them, and re-layouts: 6.94 us -> 3.24 us
    pallas_call x1 -> x0, Pallas kernels: 1.61 us -> none  [shards(): pl.pallas_call(schedule, out_shape=jax.ShapeDtypeStruct((8, TILE), jnp.in...]
where the time goes in v2:
time: 105 us
  Pallas kernels  100 us (95%)
  local copies, waits for them, and re-layouts  3.24 us (3%)
  between operations  1.29 us (1%)
    pallas_call x1, Pallas kernels, shards(): pl.pallas_call(kernel, out_shape=(jax.ShapeDtypeStruct((ROWS, F), bf16),...  100 us
    unnamed x2, local copies, waits for them, and re-layouts  3.24 us

profile of v2, /device:TPU:1, one launch (start us, length us, event | category | flops | bytes accessed | tf_op | source)
XLA Modules:
  0.0 104.8 jit_solution(9989651563914383884)
XLA Ops:
  1.3 100.3 %shard_map.86 = (bf16[256,256]{1,0:T(8,128)(2,1)}, f32[256,256]{1,0:T(8,128)}) custom-call(bf16[16,16,256]{2,1,0:T(8,128)(2,1)} %bitcast.5, bf16[256,256]{1,0:T(8,128)(2,1)} %node_ref.1, bf16[256,256]{1,0:T(8,128)(2,1)} %weight_ref.1, bf16[128,128,128]{2,1,0:T(8,128)(2,1)} %bitcast.4, s32[1,128]{1,0:T(1,128)} %bitcast.6, s32[1,128]{1,0:T(1,128)} %bitcast.7, ...), custom_call_target="tpu_custom_call" | custom-call | flops 2000000000 | bytes 5000000 | tf_op jit(solution)/shard_map/pallas_call | solution.py:394
  101.6 1.6 %copy.12 = bf16[256,256]{1,0:T(8,128)(2,1)} copy(bf16[256,256]{1,0:T(8,128)(2,1)} %get-tuple-element.4) | data formatting | bytes 262144
  103.1 1.7 %copy.13 = f32[256,256]{1,0:T(8,128)} copy(f32[256,256]{1,0:T(8,128)} %get-tuple-element.5) | data formatting | bytes 524288

commit v3 on v2

--- a/solution.py
+++ b/solution.py
@@ -17,9 +17,14 @@
 ROWS = 256
 UNIT = 16
 UNITS = ROWS // UNIT
-FIRST = (96, 112)
-ACROSS_US = 16.0
-LINK_FROM, LINK_STEPS = 12, 16
+PARTS = (
+    ((True, 96, 1), (False, 80, 1), (False, 80, -1)),
+    ((True, 112, -1), (False, 80, 1), (False, 64, -1)),
+)
+ACROSS_US, HOP_US, LEAD_US = 11.0, 3.0, 1.0
+LINK_FROM, LINK_STEPS = 48, 16
+CHAINS = 2
+SPAN = CAP // CHAINS
 
 
 def gather_edges():
@@ -36,19 +41,21 @@
         for k in range(1, half + (tie < 0)):
             edges.append((rnd, part, at(1 - k), at(-k), axis, -1))
 
-    for rnd in (0, 1):
-        tie = 1 if rnd == 0 else -1
-        chain(rnd, 0, 1, (0, 0), tie)
-        for dx in (-1, 0, 1, 2 * tie):
-            chain(rnd, 0, 0, (0, dx), 1 if dx in (0, 1) else -1)
-        chain(rnd, 1, 0, (0, 0), tie)
-        for dz in (-3, -2, -1, 0, 1, 2, 3, 4 * tie):
-            chain(rnd, 1, 1, (dz, 0), 1 if 0 <= dz <= 3 else -1)
+    for rnd, parts in enumerate(PARTS):
+        for part, (x_first, _, tie) in enumerate(parts):
+            if x_first:
+                chain(rnd, part, 1, (0, 0), tie)
+                for dx in (-1, 0, 1, 2 * tie):
+                    chain(rnd, part, 0, (0, dx), 1 if dx in (0, 1) else -1)
+            else:
+                chain(rnd, part, 0, (0, 0), tie)
+                for dz in (-3, -2, -1, 0, 1, 2, 3, 4 * tie):
+                    chain(rnd, part, 1, (dz, 0), 1 if 0 <= dz <= 3 else -1)
     return edges
 
 
 def part_rows(rnd, part):
-    return (0, FIRST[rnd]) if part == 0 else (FIRST[rnd], ROWS - FIRST[rnd])
+    return sum(rows for _, rows, _ in PARTS[rnd][:part]), PARTS[rnd][part][1]
 
 
 def gather_order(edges):
@@ -56,29 +63,52 @@
     for i, (rnd, part, frm, to, axis, way) in enumerate(edges):
         kids.setdefault((rnd, part, frm), []).append(i)
 
-    def size(i):
+    def behind(i):
         rnd, part, _, to, _, _ = edges[i]
-        return 1 + sum(size(j) for j in kids.get((rnd, part, to), []))
-
-    queue = [(0.0, 0, (0, 0, (0, 0)), -1), (0.0, 1, (0, 1, (0, 0)), -1)]
-    queue += [(ACROSS_US, 2, (1, 0, (0, 0)), -1), (ACROSS_US, 3, (1, 1, (0, 0)), -1)]
-    free, count, order = {}, 4, []
-    while queue:
-        now, _, node, via = heapq.heappop(queue)
-        starts = sorted(kids.get(node, []), key=lambda i: -size(i))
-        order.append((node, via, starts))
-        for i in starts:
-            rnd, part, _, to, axis, way = edges[i]
-            begin = max(now, free.get((axis, way), 0.0))
-            end = begin + part_rows(rnd, part)[1] * 0.01024
-            free[(axis, way)] = end
-            heapq.heappush(queue, (end + 1.0, count, (rnd, part, to), i))
-            count += 1
-    return order
+        below = [behind(j) for j in kids.get((rnd, part, to), [])]
+        return 1 + max([b[0] for b in below], default=0), 1 + sum(b[1] for b in below)
+
+    rank = [tuple(-value for value in behind(i)) for i in range(len(edges))]
+    events, count, items = [], 0, []
+
+    def at(time, node, via, link):
+        nonlocal count
+        heapq.heappush(events, (time, count, node, via, link))
+        count += 1
+
+    for rnd in range(2):
+        for part in range(len(PARTS[rnd])):
+            at(ACROSS_US * rnd, (rnd, part, (0, 0)), -1, None)
+    links = [(axis, way) for axis in (0, 1) for way in (1, -1)]
+    ready, busy = {link: [] for link in links}, {link: False for link in links}
+    while events:
+        now = events[0][0]
+        while events and events[0][0] <= now + 1e-9:
+            time, _, node, via, link = heapq.heappop(events)
+            if link is not None:
+                busy[link] = False
+                continue
+            if via < 0 or kids.get(node):
+                items.append((time, 0, len(items), node, via))
+            for i in kids.get(node, []):
+                heapq.heappush(ready[edges[i][4:]], (rank[i], i, time))
+        for link in links:
+            if ready[link] and not busy[link]:
+                _, i, since = heapq.heappop(ready[link])
+                rnd, part, _, to, _, _ = edges[i]
+                end = now + part_rows(rnd, part)[1] * 0.01024
+                busy[link] = True
+                items.append((max(since, now - LEAD_US), 1, len(items), None, i))
+                at(end, None, -1, link)
+                at(end + HOP_US, (rnd, part, to), i, None)
+    items.sort(key=lambda item: item[:3])
+    passed_on = {(rnd, part, frm) for rnd, part, frm, _, _, _ in edges}
+    last = [i for i, edge in enumerate(edges) if (edge[0], edge[1], edge[3]) not in passed_on]
+    return [item[3:] for item in items], last
 
 
 EDGES = gather_edges()
-ORDER = gather_order(EDGES)
+ORDER, LAST = gather_order(EDGES)
 
 
 def kernel(
@@ -144,14 +174,17 @@
             device_id=((nz * X + nx) * YH + yh, rep), device_id_type=MESH,
         )
 
-    def link(t, carry):
-        row = rows_ref[0, t]
-        earlier[t] = latest[row]
-        live = (t < count_ref[0, 0]).astype(jnp.int32)
-        for s in range(16):
-            now = latest[s]
-            latest[s] = now + (row == s).astype(jnp.int32) * live * (t + 1 - now)
-        return carry
+    def link(chain):
+        def step(t, carry):
+            row = rows_ref[0, t]
+            earlier[t] = latest[chain * 16 + row]
+            live = (t < count_ref[0, 0]).astype(jnp.int32)
+            for s in range(16):
+                now = latest[chain * 16 + s]
+                latest[chain * 16 + s] = now + (row == s).astype(jnp.int32) * live * (t % SPAN + 1 - now)
+            return carry
+
+        return step
 
     own_copies[0].wait()
     partner = ((u * YH) + 1 - yh, rep)
@@ -180,28 +213,30 @@
 
     node_sent = [node_copy(k, False) for k in range(1, YL)] + [node_pass(0, False)]
     sent = []
-    for step, (node, via, starts) in enumerate([entry for entry in ORDER if entry[2]]):
-        if via >= 0:
-            hop(via, True).wait_recv()
-        elif node == (1, 0, (0, 0)):
-            across(1 - yh).wait_recv()
-        for i in starts:
+    across_copy = across(yh)
+    across_copy.start()
+    for row in range(16 * CHAINS):
+        latest[row] = 0
+    for chain in range(CHAINS):
+        sums[chain, 0] = jnp.zeros((TILE, F), jnp.float32)
+    own_copies[1].wait()
+    for node, i in ORDER:
+        if node is None:
             copy = hop(i, False)
             copy.start()
             sent.append(copy)
-        if step == 1:
-            across_copy = across(yh)
-            across_copy.start()
-            own_copies[1].wait()
-            for row in range(16):
-                latest[row] = 0
-            sums[0] = jnp.zeros((TILE, F), jnp.float32)
-        elif node == (1, 1, (0, 0)):
+            share = len(sent) - LINK_FROM
+            if 0 <= share < LINK_STEPS:
+                tiles_each = CAP // LINK_STEPS
+                begin = share * tiles_each
+                lax.fori_loop(begin, begin + tiles_each, link(begin // SPAN), 0)
+        elif i >= 0:
+            hop(i, True).wait_recv()
+        elif node == (1, 0, (0, 0)):
+            across(1 - yh).wait_recv()
+        elif node == (1, len(PARTS[1]) - 1, (0, 0)):
             for copy in node_sent:
                 copy.start()
-        if LINK_FROM <= step < LINK_FROM + LINK_STEPS:
-            begin = (step - LINK_FROM) * (CAP // LINK_STEPS)
-            lax.fori_loop(begin, begin + CAP // LINK_STEPS, link, 0)
 
     for k in range(1, YL):
         node_copy(k, True).wait_recv()
@@ -213,21 +248,24 @@
     for q in range(YL * CORES):
         nodes_t[:, q * ROWS:(q + 1) * ROWS] = nodes[q].T
     own_copies[2].wait()
-    for node, via, starts in ORDER:
-        if not starts:
-            hop(via, True).wait_recv()
+    for i in LAST:
+        hop(i, True).wait_recv()
 
     def tile_step(i, carry):
-        unit = cols_ref[0, i] * (TILE // UNIT)
-        block = jnp.concatenate([grads[unit + j] for j in range(TILE // UNIT)], axis=0)
-        product = jnp.dot(tiles[i], block, preferred_element_type=jnp.float32)
-        sums[i + 1] = sums[earlier[i]] + product
-        return carry
-
-    lax.fori_loop(0, CAP, tile_step, 0, unroll=8)
+        for chain in range(CHAINS):
+            t = chain * SPAN + i
+            unit = cols_ref[0, t] * (TILE // UNIT)
+            block = jnp.concatenate([grads[unit + j] for j in range(TILE // UNIT)], axis=0)
+            product = jnp.dot(tiles[t], block, preferred_element_type=jnp.float32)
+            sums[chain, i + 1] = sums[chain, earlier[t]] + product
+        return carry
+
+    lax.fori_loop(0, SPAN, tile_step, 0, unroll=4)
 
     def take_sum(s, carry):
-        total = sums[latest[s]]
+        total = sums[0, latest[s]]
+        for chain in range(1, CHAINS):
+            total += sums[chain, latest[chain * 16 + s]]
         top = total.astype(jnp.bfloat16)
         at = pl.ds(pl.multiple_of(s * TILE, TILE), TILE)
         high[at] = top
@@ -402,7 +440,7 @@
         scratch_shapes=[
             pltpu.VMEM((PLANE * YH * UNITS, UNIT, F), bf16),
             pltpu.VMEM((CAP, TILE, TILE), bf16),
-            pltpu.VMEM((CAP + 1, TILE, F), f32),
+            pltpu.VMEM((CHAINS, SPAN + 1, TILE, F), f32),
             pltpu.VMEM((slab, F), bf16),
             pltpu.VMEM((slab, F), bf16),
             pltpu.VMEM((YL * CORES, ROWS, F), bf16),
@@ -419,7 +457,7 @@
             pltpu.VMEM((2, PLANE, 8, TILE), f32),
             pltpu.VMEM((F, F), bf16),
             pltpu.SMEM((CAP,), jnp.int32),
-            pltpu.SMEM((16,), jnp.int32),
+            pltpu.SMEM((16 * CHAINS,), jnp.int32),
             dma((4,)),
             dma((len(EDGES),)), dma((len(EDGES),)),
             dma((1,)), dma((1,)),
@@ -433,7 +471,7 @@
             dma((2,)),
         ],
         compiler_params=pltpu.CompilerParams(
-            collective_id=0, has_side_effects=True, vmem_limit_bytes=62 * 1024 * 1024
+            collective_id=0, has_side_effects=True, vmem_limit_bytes=60 * 1024 * 1024
         ),
         cost_estimate=pl.CostEstimate(flops=2_000_000_000, bytes_accessed=5_000_000, transcendentals=0),
     )(

time: 105 us -> 101 us (0.962)
  Pallas kernels: 100 us -> 96.4 us
    pallas_call x1, Pallas kernels: 100 us -> 96.4 us  [shards(): pl.pallas_call(kernel, out_shape=(jax.ShapeDtypeStruct((ROWS, F), bf16),...]
where the time goes in v3:
time: 101 us
  Pallas kernels  96.4 us (95%)
  local copies, waits for them, and re-layouts  3.24 us (3%)
  between operations  1.29 us (1%)
    pallas_call x1, Pallas kernels, shards(): pl.pallas_call(kernel, out_shape=(jax.ShapeDtypeStruct((ROWS, F), bf16),...  96.4 us
    unnamed x2, local copies, waits for them, and re-layouts  3.24 us

profile of v3, /device:TPU:1, one launch (start us, length us, event | category | flops | bytes accessed | tf_op | source)
XLA Modules:
  0.0 101.0 jit_solution(5229587864395944693)
XLA Ops:
  1.3 96.4 %shard_map.86 = (bf16[256,256]{1,0:T(8,128)(2,1)}, f32[256,256]{1,0:T(8,128)}) custom-call(bf16[16,16,256]{2,1,0:T(8,128)(2,1)} %bitcast.5, bf16[256,256]{1,0:T(8,128)(2,1)} %node_ref.1, bf16[256,256]{1,0:T(8,128)(2,1)} %weight_ref.1, bf16[128,128,128]{2,1,0:T(8,128)(2,1)} %bitcast.4, s32[1,128]{1,0:T(1,128)} %bitcast.6, s32[1,128]{1,0:T(1,128)} %bitcast.7, ...), custom_call_target="tpu_custom_call" | custom-call | flops 2000000000 | bytes 5000000 | tf_op jit(solution)/shard_map/pallas_call | solution.py:432
  97.7 1.6 %copy.12 = bf16[256,256]{1,0:T(8,128)(2,1)} copy(bf16[256,256]{1,0:T(8,128)(2,1)} %get-tuple-element.4) | data formatting | bytes 262144
  99.3 1.7 %copy.13 = f32[256,256]{1,0:T(8,128)} copy(f32[256,256]{1,0:T(8,128)} %get-tuple-element.5) | data formatting | bytes 524288

commit v4 on v3

--- a/solution.py
+++ b/solution.py
@@ -1,3 +1,4 @@
+import functools
 import heapq
 
 import jax
@@ -17,14 +18,18 @@
 ROWS = 256
 UNIT = 16
 UNITS = ROWS // UNIT
+HALF = F // 2
 PARTS = (
-    ((True, 96, 1), (False, 80, 1), (False, 80, -1)),
-    ((True, 112, -1), (False, 80, 1), (False, 64, -1)),
+    ((True, 96, 1), (False, 160, -1)),
+    ((True, 112, -1), (False, 144, 1)),
+    ((True, 96, -1), (False, 160, 1)),
+    ((True, 112, 1), (False, 144, -1)),
 )
-ACROSS_US, HOP_US, LEAD_US = 11.0, 3.0, 1.0
-LINK_FROM, LINK_STEPS = 48, 16
+START_US, HOP_US, LEAD_US = (0.0, 7.0, 0.0, 13.0), 2.0, 1.0
+LINK_FROM, LINK_STEPS = 40, 16
 CHAINS = 2
 SPAN = CAP // CHAINS
+EVERY = 3
 
 
 def gather_edges():
@@ -68,17 +73,17 @@
         below = [behind(j) for j in kids.get((rnd, part, to), [])]
         return 1 + max([b[0] for b in below], default=0), 1 + sum(b[1] for b in below)
 
-    rank = [tuple(-value for value in behind(i)) for i in range(len(edges))]
-    events, count, items = [], 0, []
+    rank = [(edges[i][0] // 2, *(-value for value in behind(i))) for i in range(len(edges))]
+    events, count, items, first_half = [], 0, [], 0.0
 
     def at(time, node, via, link):
         nonlocal count
         heapq.heappush(events, (time, count, node, via, link))
         count += 1
 
-    for rnd in range(2):
+    for rnd in range(len(PARTS)):
         for part in range(len(PARTS[rnd])):
-            at(ACROSS_US * rnd, (rnd, part, (0, 0)), -1, None)
+            at(START_US[rnd], (rnd, part, (0, 0)), -1, None)
     links = [(axis, way) for axis in (0, 1) for way in (1, -1)]
     ready, busy = {link: [] for link in links}, {link: False for link in links}
     while events:
@@ -96,11 +101,14 @@
             if ready[link] and not busy[link]:
                 _, i, since = heapq.heappop(ready[link])
                 rnd, part, _, to, _, _ = edges[i]
-                end = now + part_rows(rnd, part)[1] * 0.01024
+                end = now + part_rows(rnd, part)[1] * 0.00512
                 busy[link] = True
                 items.append((max(since, now - LEAD_US), 1, len(items), None, i))
                 at(end, None, -1, link)
                 at(end + HOP_US, (rnd, part, to), i, None)
+                if rnd < 2:
+                    first_half = max(first_half, end + HOP_US + 1.0)
+    items.append((first_half, 2, len(items), None, -1))
     items.sort(key=lambda item: item[:3])
     passed_on = {(rnd, part, frm) for rnd, part, frm, _, _, _ in edges}
     last = [i for i, edge in enumerate(edges) if (edge[0], edge[1], edge[3]) not in passed_on]
@@ -112,10 +120,10 @@
 
 
 def kernel(
-    grad_ref, node_ref, weight_ref, vals_ref, rows_ref, cols_ref, count_ref,
-    dx_ref, dw_ref,
-    grads, tiles, sums, high, low, nodes, nodes_t, sib, outgoing, incoming,
-    w_part, w_sib, w_half, w_plane, w_unit, w_y, w_full, weights, earlier, latest,
+    grad_ref, node_ref, vals_ref, rows_ref, cols_ref, count_ref,
+    result_ref, w_ref,
+    grads_0, grads_1, tiles, sums, high, low, nodes, nodes_t, sib, outgoing, incoming,
+    w_part, w_sib, w_half, w_plane, w_unit, w_full, earlier, latest,
     local_sem, gs_sem, gr_sem, ys_sem, yr_sem, ns_sem, nr_sem, ss_sem, sr_sem,
     rs_sem, rr_sem, w0_sem, p1s_sem, p1r_sem, us_sem, ur_sem, p2s_sem, p2r_sem, w4_sem,
 ):
@@ -137,11 +145,16 @@
     def rep_peer(k):
         return (me, (yl + k) % YL * CORES + core)
 
+    grads = (grads_0, grads_1)
     own_copies = [
-        pltpu.make_async_copy(grad_ref, grads.at[pl.ds(me * UNITS, UNITS)], local_sem.at[0]),
+        pltpu.make_async_copy(
+            grad_ref.at[:, :, pl.ds(0, HALF)], grads[0].at[pl.ds(me * UNITS, UNITS)], local_sem.at[0]
+        ),
         pltpu.make_async_copy(node_ref, nodes.at[rep], local_sem.at[1]),
         pltpu.make_async_copy(vals_ref, tiles, local_sem.at[2]),
-        pltpu.make_async_copy(weight_ref, weights, local_sem.at[3]),
+        pltpu.make_async_copy(
+            grad_ref.at[:, :, pl.ds(HALF, HALF)], grads[1].at[pl.ds(me * UNITS, UNITS)], local_sem.at[3]
+        ),
     ]
     for copy in own_copies:
         copy.start()
@@ -160,9 +173,9 @@
 
     def piece(rnd, part, offset):
         pz, px = (z - offset[0] + Z) % Z, (x - offset[1] + X) % X
-        py = yh if rnd == 0 else 1 - yh
+        py = yh if rnd % 2 == 0 else 1 - yh
         begin, size = part_rows(rnd, part)
-        return grads.at[pl.ds(((pz * X + px) * YH + py) * UNITS + begin // UNIT, size // UNIT)]
+        return grads[rnd // 2].at[pl.ds(((pz * X + px) * YH + py) * UNITS + begin // UNIT, size // UNIT)]
 
     def hop(i, landed):
         rnd, part, frm, to, axis, way = EDGES[i]
@@ -187,12 +200,13 @@
         return step
 
     own_copies[0].wait()
+    own_copies[3].wait()
     partner = ((u * YH) + 1 - yh, rep)
 
-    def across(index):
-        ref = grads.at[pl.ds((u * YH + index) * UNITS, UNITS)]
-        return pltpu.make_async_remote_copy(
-            src_ref=ref, dst_ref=ref, send_sem=ys_sem.at[0], recv_sem=yr_sem.at[0],
+    def across(h, index):
+        ref = grads[h].at[pl.ds((u * YH + index) * UNITS, UNITS)]
+        return pltpu.make_async_remote_copy(
+            src_ref=ref, dst_ref=ref, send_sem=ys_sem.at[h], recv_sem=yr_sem.at[h],
             device_id=partner, device_id_type=MESH,
         )
 
@@ -213,14 +227,110 @@
 
     node_sent = [node_copy(k, False) for k in range(1, YL)] + [node_pass(0, False)]
     sent = []
-    across_copy = across(yh)
-    across_copy.start()
+    across_sent = [across(h, yh) for h in range(2)]
+    for copy in across_sent:
+        copy.start()
     for row in range(16 * CHAINS):
         latest[row] = 0
     for chain in range(CHAINS):
-        sums[chain, 0] = jnp.zeros((TILE, F), jnp.float32)
+        sums[chain, 0] = jnp.zeros((TILE, HALF), jnp.float32)
     own_copies[1].wait()
+    def tile_steps(h, begin, count, unroll):
+        def step(i, carry):
+            for chain in range(CHAINS):
+                t = chain * SPAN + i
+                unit = cols_ref[0, t] * (TILE // UNIT)
+                block = jnp.concatenate([grads[h][unit + j] for j in range(TILE // UNIT)], axis=0)
+                product = jnp.dot(tiles[t], block, preferred_element_type=jnp.float32)
+                sums[chain, i + 1] = sums[chain, earlier[t]] + product
+            return carry
+
+        lax.fori_loop(begin, begin + count, step, 0, unroll=unroll)
+
+    def take_sums(h, begin, count):
+        def step(s, carry):
+            total = sums[0, latest[s]]
+            for chain in range(1, CHAINS):
+                total += sums[chain, latest[chain * 16 + s]]
+            top = total.astype(jnp.bfloat16)
+            at = pl.ds(pl.multiple_of(s * TILE, TILE), TILE)
+            high[h, at] = top
+            low[h, at] = (total - top.astype(jnp.float32)).astype(jnp.bfloat16)
+            return carry
+
+        lax.fori_loop(begin, begin + count, step, 0, unroll=2)
+
+    def block_of(index):
+        return pl.ds(pl.multiple_of(index * ROWS, ROWS), ROWS)
+
+    def sib_copy(h, k):
+        dest = (yl + k) % YL
+        return pltpu.make_async_remote_copy(
+            src_ref=high.at[h, block_of(dest * CORES + 1 - core)], dst_ref=sib.at[h, dest],
+            send_sem=ss_sem.at[h * YL + k], recv_sem=sr_sem.at[h * YL + k],
+            device_id=sibling, device_id_type=MESH,
+        )
+
+    def both(h, index, at):
+        rows = block_of(index)
+        return (
+            high[h, rows].astype(jnp.float32) + low[h, rows].astype(jnp.float32) + sib[h, at].astype(jnp.float32)
+        )
+
+    def out_copy(h, k):
+        return pltpu.make_async_remote_copy(
+            src_ref=outgoing.at[h, k], dst_ref=incoming.at[h, k],
+            send_sem=rs_sem.at[h * YL + k], recv_sem=rr_sem.at[h * YL + k],
+            device_id=rep_peer(k), device_id_type=MESH,
+        )
+
+    def sib_start(h):
+        for k in (2, 1, 3, 0):
+            sib_copy(h, k).start()
+
+    def send_block(h, k):
+        sib_copy(h, k).wait_recv()
+        dest = (yl + k) % YL
+        outgoing[h, k] = both(h, dest * CORES + core, dest).astype(jnp.bfloat16)
+        out_copy(h, k).start()
+
+    def w_dot(h, half):
+        left = nodes_t[pl.ds(pl.multiple_of(half * TILE, TILE), TILE)]
+        term = jnp.dot(left, high[h], preferred_element_type=jnp.float32)
+        term += jnp.dot(left, low[h], preferred_element_type=jnp.float32)
+        w_part[half, h * 16:(h + 1) * 16] = term.reshape(16, 8, TILE)
+
+    def node_forward():
+        for k in range(1, YL):
+            node_copy(k, True).wait_recv()
+            copy = node_pass(k, False)
+            copy.start()
+            node_sent.append(copy)
+        own_copies[2].wait()
+
+    def node_landed():
+        for k in range(YL):
+            node_pass(k, True).wait_recv()
+
+    def node_turn(q):
+        nodes_t[:, q * ROWS:(q + 1) * ROWS] = nodes[q].T
+
+    shares = [node_forward]
+    shares += [functools.partial(tile_steps, 0, begin, 4, True) for begin in range(0, SPAN, 4)]
+    shares += [functools.partial(take_sums, 0, begin, 4) for begin in range(0, 16, 4)]
+    shares += [functools.partial(sib_start, 0), node_landed]
+    shares += [functools.partial(node_turn, q) for q in range(YL * CORES)]
+    shares += [functools.partial(send_block, 0, k) for k in (2, 1, 3)]
+    shares += [functools.partial(w_dot, 0, half) for half in range(2)]
+
+    since = -1
     for node, i in ORDER:
+        if node is None and i < 0:
+            for last in LAST:
+                if EDGES[last][0] < 2:
+                    hop(last, True).wait_recv()
+            since = 0
+            continue
         if node is None:
             copy = hop(i, False)
             copy.start()
@@ -232,94 +342,32 @@
                 lax.fori_loop(begin, begin + tiles_each, link(begin // SPAN), 0)
         elif i >= 0:
             hop(i, True).wait_recv()
-        elif node == (1, 0, (0, 0)):
-            across(1 - yh).wait_recv()
-        elif node == (1, len(PARTS[1]) - 1, (0, 0)):
+        elif node[0] % 2 == 1 and node[1] == 0:
+            across(node[0] // 2, 1 - yh).wait_recv()
+        elif node == (3, len(PARTS[3]) - 1, (0, 0)):
             for copy in node_sent:
                 copy.start()
-
-    for k in range(1, YL):
-        node_copy(k, True).wait_recv()
-        copy = node_pass(k, False)
-        copy.start()
-        node_sent.append(copy)
-    for k in range(YL):
-        node_pass(k, True).wait_recv()
-    for q in range(YL * CORES):
-        nodes_t[:, q * ROWS:(q + 1) * ROWS] = nodes[q].T
-    own_copies[2].wait()
-    for i in LAST:
-        hop(i, True).wait_recv()
-
-    def tile_step(i, carry):
-        for chain in range(CHAINS):
-            t = chain * SPAN + i
-            unit = cols_ref[0, t] * (TILE // UNIT)
-            block = jnp.concatenate([grads[unit + j] for j in range(TILE // UNIT)], axis=0)
-            product = jnp.dot(tiles[t], block, preferred_element_type=jnp.float32)
-            sums[chain, i + 1] = sums[chain, earlier[t]] + product
-        return carry
-
-    lax.fori_loop(0, SPAN, tile_step, 0, unroll=4)
-
-    def take_sum(s, carry):
-        total = sums[0, latest[s]]
-        for chain in range(1, CHAINS):
-            total += sums[chain, latest[chain * 16 + s]]
-        top = total.astype(jnp.bfloat16)
-        at = pl.ds(pl.multiple_of(s * TILE, TILE), TILE)
-        high[at] = top
-        low[at] = (total - top.astype(jnp.float32)).astype(jnp.bfloat16)
-        return carry
-
-    lax.fori_loop(0, 16, take_sum, 0, unroll=2)
-
-    def block_of(index):
-        return pl.ds(pl.multiple_of(index * ROWS, ROWS), ROWS)
-
-    def sib_copy(k):
-        dest = (yl + k) % YL
-        return pltpu.make_async_remote_copy(
-            src_ref=high.at[block_of(dest * CORES + 1 - core)], dst_ref=sib.at[dest],
-            send_sem=ss_sem.at[k], recv_sem=sr_sem.at[k], device_id=sibling, device_id_type=MESH,
-        )
-
-    sib_sent = [sib_copy(k) for k in (2, 1, 3, 0)]
-    for copy in sib_sent:
-        copy.start()
-
-    def w_dot(half):
-        left = nodes_t[pl.ds(pl.multiple_of(half * TILE, TILE), TILE)]
-        term = jnp.dot(left, high[...], preferred_element_type=jnp.float32)
-        term += jnp.dot(left, low[...], preferred_element_type=jnp.float32)
-        for h in range(2):
-            w_part[half, h * 16:(h + 1) * 16] = term[:, h * TILE:(h + 1) * TILE].reshape(16, 8, TILE)
-
-    w_dot(1 - core)
+        if since >= 0:
+            if since % EVERY == 0 and shares:
+                shares.pop(0)()
+            since += 1
+    while shares:
+        shares.pop(0)()
+    for last in LAST:
+        if EDGES[last][0] >= 2:
+            hop(last, True).wait_recv()
+
+    tile_steps(1, 0, SPAN, 4)
+    take_sums(1, 0, 16)
+    sib_start(1)
+    w_dot(1, 1 - core)
     w_copy = pltpu.make_async_remote_copy(
         src_ref=w_part.at[1 - core], dst_ref=w_sib, send_sem=w0_sem.at[0], recv_sem=w0_sem.at[1],
         device_id=sibling, device_id_type=MESH,
     )
     w_copy.start()
-    w_dot(core)
-
-    def both(index, at):
-        rows = block_of(index)
-        return high[rows].astype(jnp.float32) + low[rows].astype(jnp.float32) + sib[at].astype(jnp.float32)
-
-    def out_copy(k):
-        return pltpu.make_async_remote_copy(
-            src_ref=outgoing.at[k], dst_ref=incoming.at[k], send_sem=rs_sem.at[k], recv_sem=rr_sem.at[k],
-            device_id=rep_peer(k), device_id_type=MESH,
-        )
-
-    def send_block(k):
-        sib_copy(k).wait_recv()
-        dest = (yl + k) % YL
-        outgoing[k] = both(dest * CORES + core, dest).astype(jnp.bfloat16)
-        out_copy(k).start()
-
-    send_block(2)
+    w_dot(1, core)
+    send_block(1, 2)
     w_copy.wait_recv()
     w_half[...] = w_part[core] + w_sib[...]
 
@@ -331,7 +379,7 @@
         return carry
 
     lax.fori_loop(1, PLANE, plane_send, 0)
-    for copy in sent + [across_copy] + node_sent:
+    for copy in sent + across_sent + node_sent:
         copy.wait_send()
 
     def plane_sum(k, total):
@@ -354,7 +402,7 @@
     for copy in y_sent:
         copy.start()
     for k in (1, 3):
-        send_block(k)
+        send_block(1, k)
     for k in range(1, Y):
         y_copy(k, True).wait_recv()
     total = w_unit[0]
@@ -389,28 +437,23 @@
     final = last_copy(core)
     final.start()
 
-    own_copies[3].wait()
-    sib_copy(0).wait_recv()
-    node_grad = both(rep, yl)
-    for k in range(1, YL):
-        out_copy(k).wait_recv()
-        node_grad += incoming[k].astype(jnp.float32)
-    dx_ref[...] = lax.dot_general(
-        node_grad.astype(jnp.bfloat16), weights[...], (((1,), (1,)), ((), ())),
-        preferred_element_type=jnp.float32,
-    ).astype(jnp.bfloat16)
-
+    for h in range(2):
+        sib_copy(h, 0).wait_recv()
+        node_grad = both(h, rep, yl)
+        for k in range(1, YL):
+            out_copy(h, k).wait_recv()
+            node_grad += incoming[h, k].astype(jnp.float32)
+        result_ref[:, h * HALF:(h + 1) * HALF] = node_grad.astype(jnp.bfloat16)
     last_copy(1 - core).wait_recv()
-    for half in range(2):
-        for h in range(2):
-            dw_ref[half * TILE:(half + 1) * TILE, h * TILE:(h + 1) * TILE] = (
-                w_full[half, h * 16:(h + 1) * 16].reshape(TILE, TILE)
-            )
-
-    for copy in sib_sent + [w_copy, final] + y_sent:
+    w_ref[...] = w_full[...]
+
+    for copy in [w_copy, final] + y_sent:
         copy.wait_send()
-    for k in range(1, YL):
-        out_copy(k).wait_send()
+    for h in range(2):
+        for k in range(YL):
+            sib_copy(h, k).wait_send()
+        for k in range(1, YL):
+            out_copy(h, k).wait_send()
 
     def drain(k, carry):
         pltpu.make_async_remote_copy(
@@ -423,47 +466,57 @@
     lax.fori_loop(1, PLANE, drain, 0)
 
 
+def finish(grad_ref, w_ref, weight_ref, dx_ref, dw_ref):
+    dx_ref[...] = lax.dot_general(
+        grad_ref[...], weight_ref[...], (((1,), (1,)), ((), ())), preferred_element_type=jnp.float32
+    ).astype(jnp.bfloat16)
+    for half in range(2):
+        for h in range(2):
+            dw_ref[half * TILE:(half + 1) * TILE, h * TILE:(h + 1) * TILE] = (
+                w_ref[half, h * 16:(h + 1) * 16].reshape(TILE, TILE)
+            )
+
+
 def shards(out_grad, node_input, weight, tile_vals, tile_rows, tile_cols, tile_count):
     vmem = pl.BlockSpec(memory_space=pltpu.VMEM)
     hbm = pl.BlockSpec(memory_space=pl.ANY)
     f32, bf16 = jnp.float32, jnp.bfloat16
     dma = pltpu.SemaphoreType.DMA
     slab = YL * CORES * ROWS
-    return pl.pallas_call(
+    node_grad, w_sum = pl.pallas_call(
         kernel,
         out_shape=(
             jax.ShapeDtypeStruct((ROWS, F), bf16),
-            jax.ShapeDtypeStruct((F, F), f32),
+            jax.ShapeDtypeStruct((2, PLANE, 8, TILE), f32),
         ),
-        in_specs=[hbm] * 4 + [pl.BlockSpec(memory_space=pltpu.SMEM)] * 3,
+        in_specs=[hbm] * 3 + [pl.BlockSpec(memory_space=pltpu.SMEM)] * 3,
         out_specs=(vmem, vmem),
         scratch_shapes=[
-            pltpu.VMEM((PLANE * YH * UNITS, UNIT, F), bf16),
+            pltpu.VMEM((PLANE * YH * UNITS, UNIT, HALF), bf16),
+            pltpu.VMEM((PLANE * YH * UNITS, UNIT, HALF), bf16),
             pltpu.VMEM((CAP, TILE, TILE), bf16),
-            pltpu.VMEM((CHAINS, SPAN + 1, TILE, F), f32),
-            pltpu.VMEM((slab, F), bf16),
-            pltpu.VMEM((slab, F), bf16),
+            pltpu.VMEM((CHAINS, SPAN + 1, TILE, HALF), f32),
+            pltpu.VMEM((2, slab, HALF), bf16),
+            pltpu.VMEM((2, slab, HALF), bf16),
             pltpu.VMEM((YL * CORES, ROWS, F), bf16),
             pltpu.VMEM((F, slab), bf16),
-            pltpu.VMEM((YL, ROWS, F), bf16),
-            pltpu.VMEM((YL, ROWS, F), bf16),
-            pltpu.VMEM((YL, ROWS, F), bf16),
+            pltpu.VMEM((2, YL, ROWS, HALF), bf16),
+            pltpu.VMEM((2, YL, ROWS, HALF), bf16),
+            pltpu.VMEM((2, YL, ROWS, HALF), bf16),
             pltpu.VMEM((2, PLANE, 8, TILE), f32),
             pltpu.VMEM((PLANE, 8, TILE), f32),
             pltpu.VMEM((PLANE, 8, TILE), f32),
             pltpu.VMEM((PLANE, 8, TILE), f32),
             pltpu.VMEM((Y, 8, TILE), f32),
-            pltpu.VMEM((Y, 8, TILE), f32),
             pltpu.VMEM((2, PLANE, 8, TILE), f32),
-            pltpu.VMEM((F, F), bf16),
             pltpu.SMEM((CAP,), jnp.int32),
             pltpu.SMEM((16 * CHAINS,), jnp.int32),
             dma((4,)),
             dma((len(EDGES),)), dma((len(EDGES),)),
-            dma((1,)), dma((1,)),
+            dma((2,)), dma((2,)),
             dma((2 * YL,)), dma((2 * YL,)),
-            dma((YL,)), dma((YL,)),
-            dma((YL,)), dma((YL,)),
+            dma((2 * YL,)), dma((2 * YL,)),
+            dma((2 * YL,)), dma((2 * YL,)),
             dma((2,)),
             dma((PLANE,)), dma((PLANE,)),
             dma((Y,)), dma((Y,)),
@@ -477,12 +530,21 @@
     )(
         out_grad.reshape(UNITS, UNIT, F),
         node_input,
-        weight,
         tile_vals.reshape(CAP, TILE, TILE),
         tile_rows.reshape(1, CAP),
         tile_cols.reshape(1, CAP),
         tile_count.reshape(1, 1),
     )
+    return pl.pallas_call(
+        finish,
+        out_shape=(
+            jax.ShapeDtypeStruct((ROWS, F), bf16),
+            jax.ShapeDtypeStruct((F, F), f32),
+        ),
+        in_specs=[vmem] * 3,
+        out_specs=(vmem, vmem),
+        compiler_params=pltpu.CompilerParams(vmem_limit_bytes=60 * 1024 * 1024),
+    )(node_grad, w_sum, weight)
 
 
 def solution(mesh):

time: 101 us -> 107 us (1.059)
  Pallas kernels: 96.4 us -> 105 us
  local copies, waits for them, and re-layouts: 3.24 us -> 0 us
    pallas_call x1, Pallas kernels: 96.4 us -> 103 us  [shards(): pl.pallas_call(kernel, out_shape=(jax.ShapeDtypeStruct((ROWS, F), bf16),...]
    unnamed x2 -> x0, local copies, waits for them, and re-layouts: 3.24 us -> none
    pallas_call x0 -> x1, Pallas kernels: none -> 1.93 us  [shards(): pl.pallas_call(finish, out_shape=(jax.ShapeDtypeStruct((ROWS, F), bf16),...]
where the time goes in v4:
time: 107 us
  Pallas kernels  105 us (98%)
  between operations  1.29 us (1%)
    pallas_call x1, Pallas kernels, shards(): pl.pallas_call(kernel, out_shape=(jax.ShapeDtypeStruct((ROWS, F), bf16),...  103 us

profile of v4, /device:TPU:1, one launch (start us, length us, event | category | flops | bytes accessed | tf_op | source)
XLA Modules:
  0.0 106.7 jit_solution(13170116450443669018)
XLA Ops:
  1.3 103.5 %shard_map.86 = (bf16[256,256]{1,0:T(8,128)(2,1)}, f32[2,32,8,128]{3,2,1,0:T(8,128)}) custom-call(bf16[16,16,256]{2,1,0:T(8,128)(2,1)} %bitcast.5, bf16[256,256]{1,0:T(8,128)(2,1)} %node_ref.1, bf16[128,128,128]{2,1,0:T(8,128)(2,1)} %bitcast.4, s32[1,128]{1,0:T(1,128)} %bitcast.6, s32[1,128]{1,0:T(1,128)} %bitcast.7, s32[1,1]{1,0:T(1,128)S(6)} %copy.9.count_ref), custom_call_target="tpu_custom_call" | custom-call | flops 2000000000 | bytes 5000000 | tf_op jit(solution)/shard_map/pallas_call | solution.py:486
  104.8 1.9 %shard_map.87 = (bf16[256,256]{1,0:T(8,128)(2,1)}, f32[256,256]{1,0:T(8,128)}) custom-call(bf16[256,256]{1,0:T(8,128)(2,1)} %get-tuple-element.4.grad_ref, f32[2,32,8,128]{3,2,1,0:T(8,128)} %get-tuple-element.5.w_ref, bf16[256,256]{1,0:T(8,128)(2,1)} %weight_ref.1), custom_call_target="tpu_custom_call" | custom-call | tf_op jit(solution)/shard_map/pallas_call | solution.py:538

commit v5 on v3

--- a/solution.py
+++ b/solution.py
@@ -112,10 +112,10 @@
 
 
 def kernel(
-    grad_ref, node_ref, weight_ref, vals_ref, rows_ref, cols_ref, count_ref,
-    dx_ref, dw_ref,
+    grad_ref, node_ref, vals_ref, rows_ref, cols_ref, count_ref,
+    result_ref, w_ref,
     grads, tiles, sums, high, low, nodes, nodes_t, sib, outgoing, incoming,
-    w_part, w_sib, w_half, w_plane, w_unit, w_y, w_full, weights, earlier, latest,
+    w_part, w_sib, w_half, w_plane, w_unit, w_y, w_full, earlier, latest,
     local_sem, gs_sem, gr_sem, ys_sem, yr_sem, ns_sem, nr_sem, ss_sem, sr_sem,
     rs_sem, rr_sem, w0_sem, p1s_sem, p1r_sem, us_sem, ur_sem, p2s_sem, p2r_sem, w4_sem,
 ):
@@ -141,7 +141,6 @@
         pltpu.make_async_copy(grad_ref, grads.at[pl.ds(me * UNITS, UNITS)], local_sem.at[0]),
         pltpu.make_async_copy(node_ref, nodes.at[rep], local_sem.at[1]),
         pltpu.make_async_copy(vals_ref, tiles, local_sem.at[2]),
-        pltpu.make_async_copy(weight_ref, weights, local_sem.at[3]),
     ]
     for copy in own_copies:
         copy.start()
@@ -389,23 +388,14 @@
     final = last_copy(core)
     final.start()
 
-    own_copies[3].wait()
     sib_copy(0).wait_recv()
     node_grad = both(rep, yl)
     for k in range(1, YL):
         out_copy(k).wait_recv()
         node_grad += incoming[k].astype(jnp.float32)
-    dx_ref[...] = lax.dot_general(
-        node_grad.astype(jnp.bfloat16), weights[...], (((1,), (1,)), ((), ())),
-        preferred_element_type=jnp.float32,
-    ).astype(jnp.bfloat16)
-
+    result_ref[...] = node_grad.astype(jnp.bfloat16)
     last_copy(1 - core).wait_recv()
-    for half in range(2):
-        for h in range(2):
-            dw_ref[half * TILE:(half + 1) * TILE, h * TILE:(h + 1) * TILE] = (
-                w_full[half, h * 16:(h + 1) * 16].reshape(TILE, TILE)
-            )
+    w_ref[...] = w_full[...]
 
     for copy in sib_sent + [w_copy, final] + y_sent:
         copy.wait_send()
@@ -423,19 +413,30 @@
     lax.fori_loop(1, PLANE, drain, 0)
 
 
+def finish(grad_ref, w_ref, weight_ref, dx_ref, dw_ref):
+    dx_ref[...] = lax.dot_general(
+        grad_ref[...], weight_ref[...], (((1,), (1,)), ((), ())), preferred_element_type=jnp.float32
+    ).astype(jnp.bfloat16)
+    for half in range(2):
+        for h in range(2):
+            dw_ref[half * TILE:(half + 1) * TILE, h * TILE:(h + 1) * TILE] = (
+                w_ref[half, h * 16:(h + 1) * 16].reshape(TILE, TILE)
+            )
+
+
 def shards(out_grad, node_input, weight, tile_vals, tile_rows, tile_cols, tile_count):
     vmem = pl.BlockSpec(memory_space=pltpu.VMEM)
     hbm = pl.BlockSpec(memory_space=pl.ANY)
     f32, bf16 = jnp.float32, jnp.bfloat16
     dma = pltpu.SemaphoreType.DMA
     slab = YL * CORES * ROWS
-    return pl.pallas_call(
+    node_grad, w_sum = pl.pallas_call(
         kernel,
         out_shape=(
             jax.ShapeDtypeStruct((ROWS, F), bf16),
-            jax.ShapeDtypeStruct((F, F), f32),
+            jax.ShapeDtypeStruct((2, PLANE, 8, TILE), f32),
         ),
-        in_specs=[hbm] * 4 + [pl.BlockSpec(memory_space=pltpu.SMEM)] * 3,
+        in_specs=[hbm] * 3 + [pl.BlockSpec(memory_space=pltpu.SMEM)] * 3,
         out_specs=(vmem, vmem),
         scratch_shapes=[
             pltpu.VMEM((PLANE * YH * UNITS, UNIT, F), bf16),
@@ -455,10 +456,9 @@
             pltpu.VMEM((Y, 8, TILE), f32),
             pltpu.VMEM((Y, 8, TILE), f32),
             pltpu.VMEM((2, PLANE, 8, TILE), f32),
-            pltpu.VMEM((F, F), bf16),
             pltpu.SMEM((CAP,), jnp.int32),
             pltpu.SMEM((16 * CHAINS,), jnp.int32),
-            dma((4,)),
+            dma((3,)),
             dma((len(EDGES),)), dma((len(EDGES),)),
             dma((1,)), dma((1,)),
             dma((2 * YL,)), dma((2 * YL,)),
@@ -477,12 +477,21 @@
     )(
         out_grad.reshape(UNITS, UNIT, F),
         node_input,
-        weight,
         tile_vals.reshape(CAP, TILE, TILE),
         tile_rows.reshape(1, CAP),
         tile_cols.reshape(1, CAP),
         tile_count.reshape(1, 1),
     )
+    return pl.pallas_call(
+        finish,
+        out_shape=(
+            jax.ShapeDtypeStruct((ROWS, F), bf16),
+            jax.ShapeDtypeStruct((F, F), f32),
+        ),
+        in_specs=[vmem] * 3,
+        out_specs=(vmem, vmem),
+        compiler_params=pltpu.CompilerParams(vmem_limit_bytes=60 * 1024 * 1024),
+    )(node_grad, w_sum, weight)
 
 
 def solution(mesh):

time: 101 us -> 100 us (0.990)
  local copies, waits for them, and re-layouts: 3.24 us -> 0 us
  Pallas kernels: 96.4 us -> 98.6 us
    unnamed x2 -> x0, local copies, waits for them, and re-layouts: 3.24 us -> none
    pallas_call x0 -> x1, Pallas kernels: none -> 1.93 us  [shards(): pl.pallas_call(finish, out_shape=(jax.ShapeDtypeStruct((ROWS, F), bf16),...]
where the time goes in v5:
time: 100 us; the launch traced here: 99.9 us
  Pallas kernels  98.6 us (99%)
  between operations  1.29 us (1%)
    pallas_call x1, Pallas kernels, shards(): pl.pallas_call(kernel, out_shape=(jax.ShapeDtypeStruct((ROWS, F), bf16),...  96.7 us

profile of v5, /device:TPU:1, one launch (start us, length us, event | category | flops | bytes accessed | tf_op | source)
XLA Modules:
  0.0 99.9 jit_solution(2464835277976268748)
XLA Ops:
  1.3 96.7 %shard_map.86 = (bf16[256,256]{1,0:T(8,128)(2,1)}, f32[2,32,8,128]{3,2,1,0:T(8,128)}) custom-call(bf16[16,16,256]{2,1,0:T(8,128)(2,1)} %bitcast.5, bf16[256,256]{1,0:T(8,128)(2,1)} %node_ref.1, bf16[128,128,128]{2,1,0:T(8,128)(2,1)} %bitcast.4, s32[1,128]{1,0:T(1,128)} %bitcast.6, s32[1,128]{1,0:T(1,128)} %bitcast.7, s32[1,1]{1,0:T(1,128)S(6)} %copy.9.count_ref), custom_call_target="tpu_custom_call" | custom-call | flops 2000000000 | bytes 5000000 | tf_op jit(solution)/shard_map/pallas_call | solution.py:433
  97.9 1.9 %shard_map.87 = (bf16[256,256]{1,0:T(8,128)(2,1)}, f32[256,256]{1,0:T(8,128)}) custom-call(bf16[256,256]{1,0:T(8,128)(2,1)} %get-tuple-element.4.grad_ref, f32[2,32,8,128]{3,2,1,0:T(8,128)} %get-tuple-element.5.w_ref, bf16[256,256]{1,0:T(8,128)(2,1)} %weight_ref.1), custom_call_target="tpu_custom_call" | custom-call | tf_op jit(solution)/shard_map/pallas_call | solution.py:485
